TPU v7x, 32 devices: a whole 2x2x4 slice. The times are simulated.
32 devices in a mesh: groups: 2 (over y), wide: 4 (over x, core), narrow: 4 (over z).
Axes of the slice: x: 2, y: 2, z: 4, core: 2. Of those that a mesh axis runs over, the one named last changes fastest.
Arguments:
- features: bfloat16 [8192, 768], P(('groups', 'wide')), parts along dimension 0, may hold values from -6 to 6
- self_first: bfloat16 [768, 1024], P(None, 'narrow')
- neighbor_first: bfloat16 [768, 1024], P(None, 'narrow')
- self_second: bfloat16 [1024, 1024], P(None, 'narrow')
- neighbor_second: bfloat16 [1024, 1024], P(None, 'narrow')
- adjacency: bfloat16 [288, 128, 128], P(('groups', 'wide')), parts along dimension 0, may hold values from 0 to 1, as said below
- tile_rows: int32 [288], P(('groups', 'wide')), parts along dimension 0, may hold values from 0 to 7
- tile_cols: int32 [288], P(('groups', 'wide')), parts along dimension 0, may hold values from 0 to 23, as said below
- tile_count: int32 [8], P(('groups', 'wide')), parts along dimension 0, may hold values from 12 to 32, as said below
- send_blocks: int32 [32, 4], P(('groups', 'wide')), parts along dimension 0, may hold values from 0 to 7, as said below
Outputs:
- embeddings: bfloat16 [8192, 1024], P(('groups', 'wide'), 'narrow'), parts along dimension 0
There are 2 independent parts, one for each index of `groups`. A program takes and returns all parts, laid end to end along the dimension named above; an argument that names none is the same for every part. Nothing has to cross between parts.
Inputs may be any that keep to these rules, and one draw needn't show every extreme that they name: `send_blocks`: in row p * 4 + q the entries are different blocks; the tiles of partition q read the first k of them, with k from 1 to 4 for p != q and 0 for p = q. `tile_cols`: live tiles read only slots that their sender fills. `tile_count`: each partition's live tiles stand first among its 36 slots. `adjacency`: entries are 0 or 1.
All inputs are finite; a program needn't handle non-finite values.
Results may differ from a plain program's by a relative error of at most 0.0065.
Values may be sent and summed in bfloat16 or wider, within the bound.
A program may use at most 128 MiB of HBM per device.

v0:
```python
import functools
import math

import jax
import jax.numpy as jnp
from jax import lax
from jax.experimental import pallas as pl
from jax.experimental.pallas import tpu as pltpu
from jax.sharding import PartitionSpec as P

EPSILON = 1e-06
MESH = pl.DeviceIdType.MESH
F32 = jnp.float32
BF16 = jnp.bfloat16
VMEM_LIMIT = 56 * 1024 * 1024


def dot(a, b):
    return jnp.dot(a, b, preferred_element_type=F32)


def index_kernel(num_blocks, rows_ref, cols_ref, count_ref, sb_ref, last_ref, prev_ref, out_ref):
    tiles = rows_ref.shape[0]
    width = last_ref.shape[0] // num_blocks
    partitions, slots = sb_ref.shape

    @pl.loop(0, last_ref.shape[0])
    def _(i):
        last_ref[i] = tiles

    @pl.loop(0, tiles)
    def _(t):
        prev_ref[t] = tiles

    @pl.loop(0, count_ref[0])
    def _(t):
        key = rows_ref[t] * width + cols_ref[t]
        prev_ref[t] = last_ref[key]
        last_ref[key] = t

    lane = lax.broadcasted_iota(jnp.int32, out_ref.shape[1:], 1)
    for q in range(partitions):
        value = jnp.zeros(out_ref.shape[1:], jnp.int32)
        for s in range(slots):
            value = jnp.where(lane == s, sb_ref[q, s], value)
        out_ref[q] = value


def main_kernel(
    wide,
    narrow,
    step,
    factor,
    sb_ref,
    last_ref,
    prev_ref,
    sbv_ref,
    feat_ref,
    n1_ref,
    s1_hbm,
    s2_hbm,
    n2_hbm,
    adj_hbm,
    out_ref,
    tiles,
    a,
    inv,
    s1,
    s2,
    n2,
    own1,
    halo1,
    out1,
    every,
    halo2,
    sbv_in,
    sb_in,
    pre,
    agg,
    hid,
    squares,
    part_sum,
    sums,
    load_sem,
    sb_send,
    sb_recv,
    halo_send,
    halo_recv,
    right_send,
    left_send,
    hid_recv,
    across_send,
    peer_send,
    every_recv,
    sum_send,
    sum_recv,
):
    num_blocks, blk, cols = own1.shape
    nodes = num_blocks * blk
    slots = sb_ref.shape[1]
    depth = slots * blk
    chunks = nodes // step
    per = step // blk
    pairs = wide // 2
    width = a.shape[1]
    num_tiles = prev_ref.shape[0]
    me = lax.axis_index("wide")
    n = lax.axis_index("narrow")
    pair = me // 2
    core = lax.rem(me, 2)
    other = 1 - core

    loads = [
        pltpu.make_async_copy(src, dst, load_sem.at[i])
        for i, (src, dst) in enumerate([(adj_hbm, tiles.at[pl.ds(0, num_tiles)]), (s1_hbm, s1), (n2_hbm, n2), (s2_hbm, s2)])
    ]
    for load in loads:
        load.start()

    barrier = pltpu.get_barrier_semaphore()
    for d in range(1, wide):
        pl.semaphore_signal(
            barrier, inc=1, device_id={"wide": lax.rem(me + d, wide)}, device_id_type=MESH
        )
    for d in range(1, narrow):
        pl.semaphore_signal(
            barrier, inc=1, device_id={"narrow": lax.rem(n + d, narrow)}, device_id_type=MESH
        )

    def rows_of(c):
        return pl.ds(pl.multiple_of(c * step, step), step)

    @pl.loop(0, num_blocks)
    def _(b):
        own1[b] = dot(feat_ref[pl.ds(pl.multiple_of(b * blk, blk), blk), :], n1_ref[...]).astype(BF16)

    pl.semaphore_wait(barrier, wide + narrow - 2)

    far = wide // 2
    order = [far] + [d for d in range(1, wide) if d != far]

    def sb_copy(q, p):
        return pltpu.make_async_remote_copy(
            src_ref=sbv_ref.at[q],
            dst_ref=sbv_in.at[p],
            send_sem=sb_send.at[q],
            recv_sem=sb_recv.at[p],
            device_id={"wide": q},
            device_id_type=MESH,
        )

    def halo_copy(d):
        return pltpu.make_async_remote_copy(
            src_ref=out1.at[d - 1],
            dst_ref=halo1.at[d - 1],
            send_sem=halo_send.at[d - 1],
            recv_sem=halo_recv.at[d - 1],
            device_id={"wide": lax.rem(me + d, wide)},
            device_id_type=MESH,
        )

    def halo_term(d, c):
        p = lax.rem(me + wide - d, wide)
        at = pl.ds(pl.multiple_of(nodes + p * depth, blk), depth)
        return dot(a[rows_of(c), at], halo1[d - 1])

    def hid_copy(o, c, sems, target):
        return pltpu.make_async_remote_copy(
            src_ref=hid.at[o, rows_of(c)],
            dst_ref=hid.at[o, rows_of(c)],
            send_sem=sems.at[o, c],
            recv_sem=hid_recv.at[o, c],
            device_id={"narrow": target},
            device_id_type=MESH,
        )

    def to_right(o, c):
        return hid_copy(o, c, right_send, lax.rem(n + 1, narrow))

    def to_left(o, c):
        return hid_copy(o, c, left_send, lax.rem(n + narrow - 1, narrow))

    def blocks_of(c):
        return pl.ds(c * per, per)

    def across_copy(dx, c):
        return pltpu.make_async_remote_copy(
            src_ref=every.at[0, core, blocks_of(c)],
            dst_ref=every.at[dx, core, blocks_of(c)],
            send_sem=across_send.at[dx - 1, c],
            recv_sem=every_recv.at[dx, core, c],
            device_id={"wide": lax.rem(pair + dx, pairs) * 2 + core},
            device_id_type=MESH,
        )

    def peer_copy(dx, side, c):
        return pltpu.make_async_remote_copy(
            src_ref=every.at[dx, side, blocks_of(c)],
            dst_ref=every.at[dx, side, blocks_of(c)],
            send_sem=peer_send.at[dx, c],
            recv_sem=every_recv.at[dx, side, c],
            device_id={"wide": pair * 2 + other},
            device_id_type=MESH,
        )

    def pass_on(c):
        for dx in range(1, pairs):
            across_copy(dx, c).wait_recv()
            peer_copy(dx, core, c).start()

    for d in order:
        q = lax.rem(me + d, wide)
        for s in range(slots):
            out1[d - 1, s * blk : (s + 1) * blk, :] = own1[sb_ref[q, s]]
        halo_copy(d).start()
    for d in order:
        sb_copy(lax.rem(me + d, wide), me).start()
    sbv_in[me] = sbv_ref[me]

    loads[0].wait()
    tiles[num_tiles] = jnp.zeros((blk, blk), BF16)

    @pl.loop(0, num_tiles)
    def _(t):
        tiles[t] += tiles[prev_ref[t]]

    @pl.loop(0, num_blocks)
    def _(b):
        for j in range(width // blk):
            at = pl.ds(pl.multiple_of(b * blk, blk), blk)
            a[at, j * blk : (j + 1) * blk] = tiles[last_ref[b * (width // blk) + j]]

    loads[1].wait()
    ones_tall = jnp.ones((width, blk), BF16)

    @pl.loop(0, chunks)
    def _(c):
        pre[rows_of(c), :] = dot(feat_ref[rows_of(c), :], s1[...])
        inv[rows_of(c), :] = 1.0 / jnp.maximum(dot(a[rows_of(c), :], ones_tall), 1.0)
        agg[rows_of(c), :] = dot(a[rows_of(c), 0:nodes], own1[...].reshape(nodes, cols))

    for d in order[1:] + order[:1]:
        halo_copy(d).wait_recv()
        if d != order[0]:

            @pl.loop(0, chunks)
            def _(c):
                agg[rows_of(c), :] += halo_term(d, c)

    @pl.loop(0, chunks)
    def _(c):
        mean = (agg[rows_of(c), :] + halo_term(order[0], c)) * inv[rows_of(c), 0:1]
        hid[n, rows_of(c)] = jnp.maximum(pre[rows_of(c), :] + mean, 0.0).astype(BF16)

        @pl.when(n < narrow - 1)
        def _():
            to_right(n, c).start()

        @pl.when(n > 0)
        def _():
            to_left(n, c).start()

    for d in order:
        sb_copy(me, lax.rem(me + d, wide)).wait_recv()
    to_scalar = pltpu.make_async_copy(sbv_in, sb_in, load_sem.at[4])
    to_scalar.start()
    to_scalar.wait()
    loads[2].wait()
    loads[3].wait()

    def consume(o, c, first=False):
        h = hid[o, rows_of(c)]
        at = pl.ds(pl.multiple_of(o * cols, cols), cols)
        wide_h = h.astype(F32)
        square = jnp.sum(wide_h * wide_h, axis=1, keepdims=True)
        self_term = dot(h, s2[at, :])
        neighbor_term = dot(h, n2[at, :])
        if first:
            squares[rows_of(c), :] = jnp.broadcast_to(square, (step, squares.shape[1]))
            pre[rows_of(c), :] = self_term
            agg[rows_of(c), :] = neighbor_term
        else:
            squares[rows_of(c), :] += square
            pre[rows_of(c), :] += self_term
            agg[rows_of(c), :] += neighbor_term

    @pl.loop(0, chunks)
    def _(c):
        consume(n, c, first=True)

    def finish(c):
        scale = lax.rsqrt(squares[rows_of(c), 0:1] + EPSILON)
        pre[rows_of(c), :] = pre[rows_of(c), :] * scale
        projected = (agg[rows_of(c), :] * scale).astype(BF16)
        every[0, core, blocks_of(c)] = projected.reshape(per, blk, cols)
        for dx in range(1, pairs):
            across_copy(dx, c).start()
        peer_copy(0, core, c).start()

    longest = jnp.maximum(n, narrow - 1 - n)

    @pl.loop(1, narrow)
    def _(dist):
        @pl.loop(0, chunks)
        def _(c):
            @pl.when(n >= dist)
            def _():
                to_right(n - dist, c).wait_recv()

                @pl.when(n < narrow - 1)
                def _():
                    to_right(n - dist, c).start()

            @pl.when(n + dist < narrow)
            def _():
                to_left(n + dist, c).wait_recv()

                @pl.when(n > 0)
                def _():
                    to_left(n + dist, c).start()

            @pl.when(n >= dist)
            def _():
                consume(n - dist, c)

            @pl.when(n + dist < narrow)
            def _():
                consume(n + dist, c)

            @pl.when(dist == longest)
            def _():
                finish(c)

                @pl.when(c > 0)
                def _():
                    pass_on(c - 1)

    @pl.loop(0, chunks)
    def _(c):
        agg[rows_of(c), :] = dot(a[rows_of(c), 0:nodes], every[0, core].reshape(nodes, cols))

    pass_on(chunks - 1)
    for dx in range(pairs):
        for c in range(chunks):
            peer_copy(dx, other, c).wait_recv()

    for p in range(wide):
        dx = lax.rem(pair + pairs - p // 2, pairs)
        for s in range(slots):
            at = p * depth + s * blk
            halo2[at : at + blk, :] = every[dx, p % 2, sb_in[p, 0, s]]

    ones = jnp.ones((part_sum.shape[0], cols), F32)

    @pl.loop(0, chunks)
    def _(c):
        total = agg[rows_of(c), :] + dot(a[rows_of(c), nodes:width], halo2[...])
        value = pre[rows_of(c), :] + total * inv[rows_of(c), 0:1]
        pre[rows_of(c), :] = value
        part_sum[:, rows_of(c)] = lax.dot_general(
            ones,
            value * value,
            (((1,), (1,)), ((), ())),
            precision=lax.Precision.HIGHEST,
            preferred_element_type=F32,
        )

    def sum_copy(d):
        return pltpu.make_async_remote_copy(
            src_ref=part_sum,
            dst_ref=sums.at[d - 1],
            send_sem=sum_send.at[d - 1],
            recv_sem=sum_recv.at[d - 1],
            device_id={"narrow": lax.rem(n + d, narrow)},
            device_id_type=MESH,
        )

    for d in range(1, narrow):
        sum_copy(d).start()
    for d in range(1, narrow):
        sum_copy(d).wait_recv()

    @pl.loop(0, chunks)
    def _(c):
        summed = part_sum[:, rows_of(c)]
        for d in range(1, narrow):
            summed = summed + sums[d - 1, :, rows_of(c)]
        scale = lax.rsqrt(summed + EPSILON) * factor
        turned = jnp.broadcast_to(scale[0:1, :], (blk, step)).T
        out_ref[rows_of(c), :] = (pre[rows_of(c), :] * turned[:, 0:1]).astype(BF16)

    for d in range(1, narrow):
        sum_copy(d).wait_send()
    for d in order:
        halo_copy(d).wait_send()
        sb_copy(lax.rem(me + d, wide), me).wait_send()

    @pl.loop(0, chunks)
    def _(c):
        for dx in range(1, pairs):
            across_copy(dx, c).wait_send()
            peer_copy(dx, core, c).wait_send()
        peer_copy(0, core, c).wait_send()

    @pl.loop(0, narrow)
    def _(dist):
        @pl.loop(0, chunks)
        def _(c):
            @pl.when((n >= dist) & (n < narrow - 1))
            def _():
                to_right(n - dist, c).wait_send()

            @pl.when((n + dist < narrow) & (n > 0))
            def _():
                to_left(n + dist, c).wait_send()


def shards(
    wide,
    narrow,
    features,
    self_first,
    neighbor_first,
    self_second,
    neighbor_second,
    adjacency,
    tile_rows,
    tile_cols,
    tile_count,
    send_blocks,
):
    blk = adjacency.shape[1]
    nodes, in_width = features.shape
    num_blocks = nodes // blk
    slots = send_blocks.shape[1]
    hidden_width, cols = self_second.shape
    width = nodes + wide * slots * blk
    step = 2 * blk
    chunks = nodes // step
    vmem = pl.BlockSpec(memory_space=pltpu.VMEM)
    smem = pl.BlockSpec(memory_space=pltpu.SMEM)
    anywhere = pl.BlockSpec(memory_space=pl.ANY)
    num_tiles = adjacency.shape[0]
    depth = slots * blk
    last, previous, index_rows = pl.pallas_call(
        functools.partial(index_kernel, num_blocks),
        out_shape=(
            jax.ShapeDtypeStruct((num_blocks * (width // blk),), jnp.int32),
            jax.ShapeDtypeStruct((num_tiles,), jnp.int32),
            jax.ShapeDtypeStruct((wide, 8, 128), jnp.int32),
        ),
        in_specs=[smem] * 4,
        out_specs=(smem, smem, vmem),
        name="index",
    )(tile_rows, tile_cols, tile_count, send_blocks)
    dma = pltpu.SemaphoreType.DMA
    return pl.pallas_call(
        functools.partial(main_kernel, wide, narrow, step, math.sqrt(hidden_width)),
        out_shape=jax.ShapeDtypeStruct((nodes, cols), BF16),
        in_specs=[smem] * 3 + [vmem] * 3 + [anywhere] * 4,
        out_specs=vmem,
        scratch_shapes=[
            pltpu.VMEM((num_tiles + 1, blk, blk), BF16),
            pltpu.VMEM((nodes, width), BF16),
            pltpu.VMEM((nodes, blk), F32),
            pltpu.VMEM((in_width, cols), BF16),
            pltpu.VMEM((hidden_width, cols), BF16),
            pltpu.VMEM((hidden_width, cols), BF16),
            pltpu.VMEM((num_blocks, blk, cols), BF16),
            pltpu.VMEM((wide - 1, depth, cols), BF16),
            pltpu.VMEM((wide - 1, depth, cols), BF16),
            pltpu.VMEM((wide // 2, 2, num_blocks, blk, cols), BF16),
            pltpu.VMEM((wide * depth, cols), BF16),
            pltpu.VMEM((wide, 8, 128), jnp.int32),
            pltpu.SMEM((wide, 8, 128), jnp.int32),
            pltpu.VMEM((nodes, cols), F32),
            pltpu.VMEM((nodes, cols), F32),
            pltpu.VMEM((narrow, nodes, cols), BF16),
            pltpu.VMEM((nodes, 128), F32),
            pltpu.VMEM((8, nodes), F32),
            pltpu.VMEM((narrow - 1, 8, nodes), F32),
            dma((5,)),
            dma((wide,)),
            dma((wide,)),
            dma((wide - 1,)),
            dma((wide - 1,)),
            dma((narrow, chunks)),
            dma((narrow, chunks)),
            dma((narrow, chunks)),
            dma((wide // 2 - 1, chunks)),
            dma((wide // 2, chunks)),
            dma((wide // 2, 2, chunks)),
            dma((narrow - 1,)),
            dma((narrow - 1,)),
        ],
        compiler_params=pltpu.CompilerParams(
            collective_id=0, has_side_effects=True, vmem_limit_bytes=VMEM_LIMIT
        ),
        name="layers",
    )(
        send_blocks,
        last,
        previous,
        index_rows,
        features,
        neighbor_first,
        self_first,
        self_second,
        neighbor_second,
        adjacency,
    )


def solution(mesh):
    in_specs = (
        P(("groups", "wide"), None),
        P(None, "narrow"),
        P(None, "narrow"),
        P(None, "narrow"),
        P(None, "narrow"),
        P(("groups", "wide"), None, None),
        P(("groups", "wide")),
        P(("groups", "wide")),
        P(("groups", "wide")),
        P(("groups", "wide"), None),
    )
    out_specs = P(("groups", "wide"), "narrow")
    body = functools.partial(shards, mesh.shape["wide"], mesh.shape["narrow"])
    return jax.shard_map(body, mesh=mesh, in_specs=in_specs, out_specs=out_specs, check_vma=False)
```

profile of v0, /device:TPU:1, one launch (start us, length us, event | category | flops | bytes accessed | tf_op | source)
XLA Modules:
  0.0 78.3 jit_solution(804399245921921769)
XLA Ops:
  0.7 3.1 %index.1 = (s32[192]{0:T(256)}, s32[36]{0:T(128)}, s32[4,8,128]{2,1,0:T(8,128)}) custom-call(s32[36]{0:T(128)} %rows_ref.1, s32[36]{0:T(128)} %cols_ref.1, s32[1]{0:T(128)S(6)} %copy.12.count_ref, s32[4,4]{1,0:T(4,128)} %sb_ref.3), custom_call_target="tpu_custom_call" | custom-call | tf_op jit(solution)/shard_map/index/pallas_call | solution.py:445
  3.7 72.7 %layers.1 = bf16[1024,256]{1,0:T(8,128)(2,1)} custom-call(s32[4,4]{1,0:T(4,128)} %sb_ref.3, s32[192]{0:T(256)} %get-tuple-element.8.last_ref, s32[36]{0:T(128)} %get-tuple-element.9.prev_ref, s32[4,8,128]{2,1,0:T(8,128)} %get-tuple-element.10.sbv_ref, bf16[1024,768]{1,0:T(8,128)(2,1)} %feat_ref.1, bf16[768,256]{1,0:T(8,128)(2,1)} %n1_ref.1, ...), custom_call_target="tpu_custom_call" | custom-call | tf_op jit(solution)/shard_map/layers/pallas_call | solution.py:457
  76.5 1.9 %copy.13 = bf16[1024,256]{1,0:T(8,128)(2,1)} copy(bf16[1024,256]{1,0:T(8,128)(2,1)} %layers.1) | data formatting | bytes 1048576
where the time goes:
time: 78.3 us
  Pallas kernels  75.8 us (97%)
  local copies, waits for them, and re-layouts  1.87 us (2%)
    pallas_call x1, Pallas kernels, shards(): pl.pallas_call(functools.partial(main_kernel, wide, narrow, step, math.sq...  72.7 us
    pallas_call x1, Pallas kernels, shards(): pl.pallas_call(functools.partial(index_kernel, num_blocks), out_shape=(ja...  3.08 us
    unnamed x1, local copies, waits for them, and re-layouts  1.87 us

commit v1 on v0

--- a/solution.py
+++ b/solution.py
@@ -19,49 +19,24 @@
     return jnp.dot(a, b, preferred_element_type=F32)
 
 
-def index_kernel(num_blocks, rows_ref, cols_ref, count_ref, sb_ref, last_ref, prev_ref, out_ref):
-    tiles = rows_ref.shape[0]
-    width = last_ref.shape[0] // num_blocks
-    partitions, slots = sb_ref.shape
-
-    @pl.loop(0, last_ref.shape[0])
-    def _(i):
-        last_ref[i] = tiles
-
-    @pl.loop(0, tiles)
-    def _(t):
-        prev_ref[t] = tiles
-
-    @pl.loop(0, count_ref[0])
-    def _(t):
-        key = rows_ref[t] * width + cols_ref[t]
-        prev_ref[t] = last_ref[key]
-        last_ref[key] = t
-
-    lane = lax.broadcasted_iota(jnp.int32, out_ref.shape[1:], 1)
-    for q in range(partitions):
-        value = jnp.zeros(out_ref.shape[1:], jnp.int32)
-        for s in range(slots):
-            value = jnp.where(lane == s, sb_ref[q, s], value)
-        out_ref[q] = value
-
-
 def main_kernel(
     wide,
     narrow,
     step,
     factor,
     sb_ref,
-    last_ref,
-    prev_ref,
-    sbv_ref,
-    feat_ref,
-    n1_ref,
+    rows_ref,
+    cols_ref,
+    count_ref,
+    feat_hbm,
+    n1_hbm,
     s1_hbm,
     s2_hbm,
     n2_hbm,
     adj_hbm,
     out_ref,
+    feat_ref,
+    n1_ref,
     tiles,
     a,
     inv,
@@ -73,6 +48,9 @@
     out1,
     every,
     halo2,
+    table,
+    table_in,
+    sbv_ref,
     sbv_in,
     sb_in,
     pre,
@@ -103,16 +81,18 @@
     per = step // blk
     pairs = wide // 2
     width = a.shape[1]
-    num_tiles = prev_ref.shape[0]
+    num_tiles = rows_ref.shape[0]
     me = lax.axis_index("wide")
     n = lax.axis_index("narrow")
     pair = me // 2
     core = lax.rem(me, 2)
     other = 1 - core
 
+    sources = [feat_hbm, n1_hbm, adj_hbm, s1_hbm, n2_hbm, s2_hbm]
+    targets = [feat_ref, n1_ref, tiles.at[pl.ds(0, num_tiles)], s1, n2, s2]
     loads = [
         pltpu.make_async_copy(src, dst, load_sem.at[i])
-        for i, (src, dst) in enumerate([(adj_hbm, tiles.at[pl.ds(0, num_tiles)]), (s1_hbm, s1), (n2_hbm, n2), (s2_hbm, s2)])
+        for i, (src, dst) in enumerate(zip(sources, targets))
     ]
     for load in loads:
         load.start()
@@ -126,6 +106,16 @@
         pl.semaphore_signal(
             barrier, inc=1, device_id={"narrow": lax.rem(n + d, narrow)}, device_id_type=MESH
         )
+
+    lane = lax.broadcasted_iota(jnp.int32, (8, 128), 1)
+    for q in range(wide):
+        value = jnp.zeros((8, 128), jnp.int32)
+        for s in range(slots):
+            value = jnp.where(lane == s, sb_ref[q, s], value)
+        sbv_ref[q] = value
+
+    loads[0].wait()
+    loads[1].wait()
 
     def rows_of(c):
         return pl.ds(pl.multiple_of(c * step, step), step)
@@ -217,20 +207,50 @@
         sb_copy(lax.rem(me + d, wide), me).start()
     sbv_in[me] = sbv_ref[me]
 
-    loads[0].wait()
+    block_row = lax.broadcasted_iota(jnp.int32, (num_blocks, 128), 0)
+    block_col = lax.broadcasted_iota(jnp.int32, (num_blocks, 128), 1)
+    live = count_ref[0]
+
+    def key_of(t):
+        return jnp.where(t < live, rows_ref[t] * 128 + cols_ref[t], -1 - t)
+
+    def gather_keys(t, keys):
+        return jnp.where(lane == t, key_of(t), keys)
+
+    keys = lax.fori_loop(0, num_tiles, gather_keys, jnp.full((8, 128), -1000, jnp.int32))
+
+    def link(t, state):
+        last, prev = state
+        key = key_of(t)
+        last = jnp.where(block_row * 128 + block_col == key, t, last)
+        prev = jnp.where((keys == key) & (lane > t), t, prev)
+        return last, prev
+
+    empty = (
+        jnp.full((num_blocks, 128), num_tiles, jnp.int32),
+        jnp.full((8, 128), num_tiles, jnp.int32),
+    )
+    last, prev = lax.fori_loop(0, num_tiles, link, empty)
+    table[0:num_blocks, :] = last
+    table[num_blocks : num_blocks + 8, :] = prev
+    to_scalar = pltpu.make_async_copy(table, table_in, load_sem.at[7])
+    to_scalar.start()
+    to_scalar.wait()
+
+    loads[2].wait()
     tiles[num_tiles] = jnp.zeros((blk, blk), BF16)
 
     @pl.loop(0, num_tiles)
     def _(t):
-        tiles[t] += tiles[prev_ref[t]]
+        tiles[t] += tiles[table_in[num_blocks, t]]
 
     @pl.loop(0, num_blocks)
     def _(b):
         for j in range(width // blk):
             at = pl.ds(pl.multiple_of(b * blk, blk), blk)
-            a[at, j * blk : (j + 1) * blk] = tiles[last_ref[b * (width // blk) + j]]
-
-    loads[1].wait()
+            a[at, j * blk : (j + 1) * blk] = tiles[table_in[b, j]]
+
+    loads[3].wait()
     ones_tall = jnp.ones((width, blk), BF16)
 
     @pl.loop(0, chunks)
@@ -262,11 +282,11 @@
 
     for d in order:
         sb_copy(me, lax.rem(me + d, wide)).wait_recv()
-    to_scalar = pltpu.make_async_copy(sbv_in, sb_in, load_sem.at[4])
+    to_scalar = pltpu.make_async_copy(sbv_in, sb_in, load_sem.at[6])
     to_scalar.start()
     to_scalar.wait()
-    loads[2].wait()
-    loads[3].wait()
+    loads[4].wait()
+    loads[5].wait()
 
     def consume(o, c, first=False):
         h = hid[o, rows_of(c)]
@@ -350,20 +370,13 @@
             at = p * depth + s * blk
             halo2[at : at + blk, :] = every[dx, p % 2, sb_in[p, 0, s]]
 
-    ones = jnp.ones((part_sum.shape[0], cols), F32)
-
     @pl.loop(0, chunks)
     def _(c):
         total = agg[rows_of(c), :] + dot(a[rows_of(c), nodes:width], halo2[...])
         value = pre[rows_of(c), :] + total * inv[rows_of(c), 0:1]
         pre[rows_of(c), :] = value
-        part_sum[:, rows_of(c)] = lax.dot_general(
-            ones,
-            value * value,
-            (((1,), (1,)), ((), ())),
-            precision=lax.Precision.HIGHEST,
-            preferred_element_type=F32,
-        )
+        row_sum = jnp.sum(value * value, axis=1, keepdims=True)
+        part_sum[:, rows_of(c)] = jnp.broadcast_to(row_sum, (step, blk)).T[0:8, :]
 
     def sum_copy(d):
         return pltpu.make_async_remote_copy(
@@ -442,24 +455,15 @@
     anywhere = pl.BlockSpec(memory_space=pl.ANY)
     num_tiles = adjacency.shape[0]
     depth = slots * blk
-    last, previous, index_rows = pl.pallas_call(
-        functools.partial(index_kernel, num_blocks),
-        out_shape=(
-            jax.ShapeDtypeStruct((num_blocks * (width // blk),), jnp.int32),
-            jax.ShapeDtypeStruct((num_tiles,), jnp.int32),
-            jax.ShapeDtypeStruct((wide, 8, 128), jnp.int32),
-        ),
-        in_specs=[smem] * 4,
-        out_specs=(smem, smem, vmem),
-        name="index",
-    )(tile_rows, tile_cols, tile_count, send_blocks)
     dma = pltpu.SemaphoreType.DMA
     return pl.pallas_call(
         functools.partial(main_kernel, wide, narrow, step, math.sqrt(hidden_width)),
         out_shape=jax.ShapeDtypeStruct((nodes, cols), BF16),
-        in_specs=[smem] * 3 + [vmem] * 3 + [anywhere] * 4,
+        in_specs=[smem] * 4 + [anywhere] * 6,
         out_specs=vmem,
         scratch_shapes=[
+            pltpu.VMEM((nodes, in_width), BF16),
+            pltpu.VMEM((in_width, cols), BF16),
             pltpu.VMEM((num_tiles + 1, blk, blk), BF16),
             pltpu.VMEM((nodes, width), BF16),
             pltpu.VMEM((nodes, blk), F32),
@@ -471,6 +475,9 @@
             pltpu.VMEM((wide - 1, depth, cols), BF16),
             pltpu.VMEM((wide // 2, 2, num_blocks, blk, cols), BF16),
             pltpu.VMEM((wide * depth, cols), BF16),
+            pltpu.VMEM((num_blocks + 8, 128), jnp.int32),
+            pltpu.SMEM((num_blocks + 8, 128), jnp.int32),
+            pltpu.VMEM((wide, 8, 128), jnp.int32),
             pltpu.VMEM((wide, 8, 128), jnp.int32),
             pltpu.SMEM((wide, 8, 128), jnp.int32),
             pltpu.VMEM((nodes, cols), F32),
@@ -479,7 +486,7 @@
             pltpu.VMEM((nodes, 128), F32),
             pltpu.VMEM((8, nodes), F32),
             pltpu.VMEM((narrow - 1, 8, nodes), F32),
-            dma((5,)),
+            dma((8,)),
             dma((wide,)),
             dma((wide,)),
             dma((wide - 1,)),
@@ -499,9 +506,9 @@
         name="layers",
     )(
         send_blocks,
-        last,
-        previous,
-        index_rows,
+        tile_rows,
+        tile_cols,
+        tile_count,
         features,
         neighbor_first,
         self_first,

time: 78.3 us -> 73.3 us (0.936)
  Pallas kernels: 75.8 us -> 70.5 us
    pallas_call x1 -> x0, Pallas kernels: 3.08 us -> none  [shards(): pl.pallas_call(functools.partial(index_kernel, num_blocks), out_shape=(ja...]
    pallas_call x1, Pallas kernels: 72.7 us -> 70.5 us  [shards(): pl.pallas_call(functools.partial(main_kernel, wide, narrow, step, math.sq...]
where the time goes in v1:
time: 73.3 us; the launch traced here: 73.1 us
  Pallas kernels  70.5 us (96%)
  local copies, waits for them, and re-layouts  1.87 us (3%)
    pallas_call x1, Pallas kernels, shards(): pl.pallas_call(functools.partial(main_kernel, wide, narrow, step, math.sq...  70.5 us
    unnamed x1, local copies, waits for them, and re-layouts  1.87 us

profile of v1, /device:TPU:1, one launch (start us, length us, event | category | flops | bytes accessed | tf_op | source)
XLA Modules:
  0.0 73.1 jit_solution(7364619326825365716)
XLA Ops:
  0.7 70.5 %layers.1 = bf16[1024,256]{1,0:T(8,128)(2,1)} custom-call(s32[4,4]{1,0:T(4,128)} %sb_ref.1, s32[36]{0:T(128)} %rows_ref.1, s32[36]{0:T(128)} %cols_ref.1, s32[1]{0:T(128)S(6)} %copy.12.count_ref, bf16[1024,768]{1,0:T(8,128)(2,1)} %feat_hbm.1, bf16[768,256]{1,0:T(8,128)(2,1)} %n1_hbm.1, bf16[768,256]{1,0:T(8,128)(2,1)} %s1_hbm.1, bf16[1024,256]{1,0:T(8,128)(2,1)} %s2_hbm.1, ...), custom_call_target="tpu_custom_call" | custom-call | tf_op jit(solution)/shard_map/layers/pallas_call | solution.py:459
  71.2 1.9 %copy.13 = bf16[1024,256]{1,0:T(8,128)(2,1)} copy(bf16[1024,256]{1,0:T(8,128)(2,1)} %layers.1) | data formatting | bytes 1048576

commit v2 on v1

--- a/solution.py
+++ b/solution.py
@@ -120,9 +120,10 @@
     def rows_of(c):
         return pl.ds(pl.multiple_of(c * step, step), step)
 
-    @pl.loop(0, num_blocks)
+    @pl.loop(0, num_blocks // 4)
     def _(b):
-        own1[b] = dot(feat_ref[pl.ds(pl.multiple_of(b * blk, blk), blk), :], n1_ref[...]).astype(BF16)
+        at = pl.ds(pl.multiple_of(b * (4 * blk), blk), 4 * blk)
+        own1[pl.ds(b * 4, 4)] = dot(feat_ref[at, :], n1_ref[...]).astype(BF16).reshape(4, blk, cols)
 
     pl.semaphore_wait(barrier, wide + narrow - 2)
 
@@ -351,14 +352,15 @@
             def _():
                 finish(c)
 
-                @pl.when(c > 0)
+                @pl.when(c > 1)
                 def _():
-                    pass_on(c - 1)
+                    pass_on(c - 2)
 
     @pl.loop(0, chunks)
     def _(c):
         agg[rows_of(c), :] = dot(a[rows_of(c), 0:nodes], every[0, core].reshape(nodes, cols))
 
+    pass_on(chunks - 2)
     pass_on(chunks - 1)
     for dx in range(pairs):
         for c in range(chunks):
@@ -370,13 +372,10 @@
             at = p * depth + s * blk
             halo2[at : at + blk, :] = every[dx, p % 2, sb_in[p, 0, s]]
 
-    @pl.loop(0, chunks)
-    def _(c):
-        total = agg[rows_of(c), :] + dot(a[rows_of(c), nodes:width], halo2[...])
-        value = pre[rows_of(c), :] + total * inv[rows_of(c), 0:1]
-        pre[rows_of(c), :] = value
-        row_sum = jnp.sum(value * value, axis=1, keepdims=True)
-        part_sum[:, rows_of(c)] = jnp.broadcast_to(row_sum, (step, blk)).T[0:8, :]
+    value = pre[...] + (agg[...] + dot(a[:, nodes:width], halo2[...])) * inv[:, 0:1]
+    pre[...] = value
+    row_sum = jnp.sum(value * value, axis=1, keepdims=True)
+    part_sum[...] = jnp.broadcast_to(row_sum, (nodes, blk)).T[0:8, :]
 
     def sum_copy(d):
         return pltpu.make_async_remote_copy(

time: 73.3 us -> 71.5 us (0.975)
  Pallas kernels: 70.5 us -> 68.8 us
    pallas_call x1, Pallas kernels: 70.5 us -> 68.8 us  [shards(): pl.pallas_call(functools.partial(main_kernel, wide, narrow, step, math.sq...]
where the time goes in v2:
time: 71.5 us; the launch traced here: 71.3 us
  Pallas kernels  68.8 us (96%)
  local copies, waits for them, and re-layouts  1.87 us (3%)
    pallas_call x1, Pallas kernels, shards(): pl.pallas_call(functools.partial(main_kernel, wide, narrow, step, math.sq...  68.8 us
    unnamed x1, local copies, waits for them, and re-layouts  1.87 us

profile of v2, /device:TPU:1, one launch (start us, length us, event | category | flops | bytes accessed | tf_op | source)
XLA Modules:
  0.0 71.3 jit_solution(11506651125305256530)
XLA Ops:
  0.7 68.8 %layers.1 = bf16[1024,256]{1,0:T(8,128)(2,1)} custom-call(s32[4,4]{1,0:T(4,128)} %sb_ref.1, s32[36]{0:T(128)} %rows_ref.1, s32[36]{0:T(128)} %cols_ref.1, s32[1]{0:T(128)S(6)} %copy.12.count_ref, bf16[1024,768]{1,0:T(8,128)(2,1)} %feat_hbm.1, bf16[768,256]{1,0:T(8,128)(2,1)} %n1_hbm.1, bf16[768,256]{1,0:T(8,128)(2,1)} %s1_hbm.1, bf16[1024,256]{1,0:T(8,128)(2,1)} %s2_hbm.1, ...), custom_call_target="tpu_custom_call" | custom-call | tf_op jit(solution)/shard_map/layers/pallas_call | solution.py:458
  69.5 1.9 %copy.13 = bf16[1024,256]{1,0:T(8,128)(2,1)} copy(bf16[1024,256]{1,0:T(8,128)(2,1)} %layers.1) | data formatting | bytes 1048576

commit v3 on v2

--- a/solution.py
+++ b/solution.py
@@ -356,11 +356,9 @@
                 def _():
                     pass_on(c - 2)
 
-    @pl.loop(0, chunks)
-    def _(c):
-        agg[rows_of(c), :] = dot(a[rows_of(c), 0:nodes], every[0, core].reshape(nodes, cols))
-
     pass_on(chunks - 2)
+    agg[...] = dot(a[:, 0:nodes], every[0, core].reshape(nodes, cols))
+
     pass_on(chunks - 1)
     for dx in range(pairs):
         for c in range(chunks):

time: 71.5 us -> 72.1 us (level)
  no operation moved by 1% of the time
where the time goes in v3:
time: 72.1 us; the launch traced here: 71.9 us
  Pallas kernels  69.3 us (96%)
  local copies, waits for them, and re-layouts  1.87 us (3%)
    pallas_call x1, Pallas kernels, shards(): pl.pallas_call(functools.partial(main_kernel, wide, narrow, step, math.sq...  69.3 us
    unnamed x1, local copies, waits for them, and re-layouts  1.87 us

profile of v3, /device:TPU:1, one launch (start us, length us, event | category | flops | bytes accessed | tf_op | source)
XLA Modules:
  0.0 71.9 jit_solution(3761173299183266511)
XLA Ops:
  0.7 69.3 %layers.1 = bf16[1024,256]{1,0:T(8,128)(2,1)} custom-call(s32[4,4]{1,0:T(4,128)} %sb_ref.1, s32[36]{0:T(128)} %rows_ref.1, s32[36]{0:T(128)} %cols_ref.1, s32[1]{0:T(128)S(6)} %copy.12.count_ref, bf16[1024,768]{1,0:T(8,128)(2,1)} %feat_hbm.1, bf16[768,256]{1,0:T(8,128)(2,1)} %n1_hbm.1, bf16[768,256]{1,0:T(8,128)(2,1)} %s1_hbm.1, bf16[1024,256]{1,0:T(8,128)(2,1)} %s2_hbm.1, ...), custom_call_target="tpu_custom_call" | custom-call | tf_op jit(solution)/shard_map/layers/pallas_call | solution.py:456
  70.0 1.9 %copy.13 = bf16[1024,256]{1,0:T(8,128)(2,1)} copy(bf16[1024,256]{1,0:T(8,128)(2,1)} %layers.1) | data formatting | bytes 1048576
